TPU v7x, 256 devices: a whole 4x4x8 slice. The times are simulated.
256 devices in a mesh: blk: 32 (over y_lo, z, core), inner: 8 (over y_hi, x).
Axes of the slice: x: 4, y: 4 (y_hi: 2, y_lo: 2; y = y_hi * 2 + y_lo), z: 8, core: 2. Of those that a mesh axis runs over, the one named last changes fastest.
Arguments:
- queries: bfloat16 [6144, 5120], P('blk', 'inner'), may hold values from -48 to 48
- keys: bfloat16 [6144, 1024], P('blk', 'inner'), may hold values from -48 to 48
- values: bfloat16 [6144, 1024], P('blk', 'inner'), may hold values from -6 to 6
- positions: int32 [6144], P('blk'), may hold values from 0 to 6143, as said below
- out_weight: bfloat16 [5120, 5120], P('inner'), may hold values from -0.078125 to 0.078125
Outputs:
- projected: bfloat16 [6144, 5120], P(('blk', 'inner'))
Inputs may be any that keep to these rules, and one draw needn't show every extreme that they name: The rows of index b of blk (rows 192 b to 192 b + 191) hold the positions c * 96 to c * 96 + 95 followed by (63 - c) * 96 to (63 - c) * 96 + 95, in increasing order, with a different c from 0 to 31 for every b; every position appears once.
All inputs are finite; a program needn't handle non-finite values.
Results may differ from a plain program's by a relative error of at most 0.018.
Values may be sent and summed in bfloat16 or wider, within the bound.
A program may use at most 128 MiB of HBM per device.

v0:
```python
import math

import jax
import jax.numpy as jnp
from jax import lax
from jax.sharding import PartitionSpec as P

HEAD_WIDTH = 128
QUERY_PER_KEY = 5


def initial_state(head_count, query_count):
    highest = jnp.full((head_count, QUERY_PER_KEY, query_count), -1e30, jnp.float32)
    totals = jnp.zeros((head_count, QUERY_PER_KEY, query_count), jnp.float32)
    summed = jnp.zeros((head_count, QUERY_PER_KEY, query_count, HEAD_WIDTH), jnp.float32)
    return (highest, totals, summed)


def attend(running, query_rows, query_pos, key_rows, value_rows, key_pos, block_size):
    highest, totals, summed = running
    inverse_root = 1.0 / math.sqrt(HEAD_WIDTH)
    head_count = key_rows.shape[1] // HEAD_WIDTH
    key_count = key_rows.shape[0]
    for offset in range(0, key_count, block_size):
        block_rows = min(block_size, key_count - offset)
        key_block = key_rows[offset : offset + block_rows].reshape(
            block_rows, head_count, HEAD_WIDTH
        )
        value_block = value_rows[offset : offset + block_rows].reshape(
            block_rows, head_count, HEAD_WIDTH
        )
        visible = key_pos[offset : offset + block_rows][None, :] <= query_pos[:, None]
        scores = (
            jnp.einsum("qhgd,khd->hgqk", query_rows, key_block, preferred_element_type=jnp.float32)
            * inverse_root
        )
        scores = jnp.where(visible[None, None], scores, -1e30)
        new_high = jnp.maximum(highest, jnp.max(scores, axis=-1))
        rescale = jnp.exp(highest - new_high)
        weights = jnp.where(visible[None, None], jnp.exp(scores - new_high[..., None]), 0.0)
        totals = totals * rescale + jnp.sum(weights, axis=-1)
        summed = summed * rescale[..., None] + jnp.einsum(
            "hgqk,khd->hgqd",
            weights.astype(jnp.bfloat16),
            value_block,
            preferred_element_type=jnp.float32,
        )
        highest = new_high
    return (highest, totals, summed)


def finish(totals, summed):
    mixed = (summed / totals[..., None]).astype(jnp.bfloat16)
    query_count = mixed.shape[2]
    return jnp.transpose(mixed, (2, 0, 1, 3)).reshape(
        query_count, mixed.shape[0] * QUERY_PER_KEY * HEAD_WIDTH
    )


def shards(queries, keys, values, positions, out_weight):
    own_rows = queries.shape[0]
    head_count = keys.shape[1] // HEAD_WIDTH
    query_rows = queries.reshape(own_rows, head_count, QUERY_PER_KEY, HEAD_WIDTH)
    start_states = initial_state(head_count, own_rows)
    folded = attend(
        start_states,
        query_rows,
        positions,
        lax.all_gather(keys, "blk", axis=0, tiled=True),
        lax.all_gather(values, "blk", axis=0, tiled=True),
        lax.all_gather(positions, "blk", axis=0, tiled=True),
        512,
    )
    attended_values = finish(folded[1], folded[2])
    return lax.psum_scatter(
        jnp.dot(attended_values, out_weight, preferred_element_type=jnp.float32).astype(
            jnp.bfloat16
        ),
        "inner",
        scatter_dimension=0,
        tiled=True,
    )


def solution(mesh):
    placed = (P("blk", "inner"), P("blk", "inner"), P("blk", "inner"), P("blk"), P("inner", None))
    return jax.shard_map(
        shards, mesh=mesh, in_specs=placed, out_specs=P(("blk", "inner"), None), check_vma=False
    )
```

profile of v0, /device:TPU:24, one launch (start us, length us, event | category | flops | bytes accessed | tf_op | source)
XLA Modules:
  0.0 251.9 jit_solution(523057684553220909)
XLA Ops:
  8.1 1.3 dynamic-slice
  10.0 0.9 dynamic-update-slice
  10.9 110.1 %all-reduce = s32[6144]{0:T(1024)S(1)} all-reduce(s32[6144]{0:T(1024)S(1)} %dynamic-update-slice), channel_id=1, replica_groups=mesh['blk'=32,'inner'=8] {'blk'}, use_global_device_ids=true, to_apply=%add | all-reduce | flops 6144 | bytes 49152
  121.0 1.1 copy.18
  122.2 1.5 broadcast_compare_fusion.10
  123.7 1.7 fusion.11
  133.1 1.4 fusion.12
  134.5 1.4 fusion.16
  135.9 1.6 fusion.20
  137.5 1.4 fusion.24
  138.9 1.4 fusion.28
  140.2 1.4 fusion.32
  141.7 2.4 fusion.47
  145.1 0.8 copy-done.17
  148.2 0.8 copy-done.13
  149.7 0.8 copy-done.11
  151.3 0.8 copy-done.9
  152.8 0.8 copy-done.7
  154.4 0.8 copy-done.5
  155.9 0.8 copy-done.3
  157.5 0.8 copy-done.1
  158.3 0.9 fusion.37
  160.1 5.9 %convolution_convert_fusion = bf16[192,5120]{1,0:T(8,128)(2,1)} fusion(bf16[192,640]{0,1:T(8,128)(2,1)S(1)} %bitcast.345, bf16[640,5120]{1,0:T(8,128)(2,1)} %param.9), kind=kOutput, calls=%fused_computation | convolution fusion | flops 1259274240 | bytes 8765440 | tf_op jit(solution)/shard_map/dot_general | solution.py:76
  166.1 79.3 %reduce-scatter.2.cloned.1.call-done = bf16[24,5120]{1,0:T(8,128)(2,1)} async-done(((bf16[192,5120]{1,0:T(8,128)(2,1)}), bf16[24,5120]{1,0:T(8,128)(2,1)}) %reduce-scatter.2.cloned.1.call-update) | async-done | bytes 245776 | tf_op jit(solution)/shard_map/reduce_scatter | solution.py:75
  (72 shorter events, 17.6 us)
Async XLA Ops:
  6.5 117.1 %all-gather.3.cloned.1.call-start = ((), (), s32[]{:S(2)}) async-start(), calls=%async_computation.1 | async-start | bytes 1622016 | tf_op jit(solution)/shard_map/all_gather | solution.py:69
  7.3 134.5 %all-gather.5.cloned.1.call-start = ((), (), s32[]{:S(2)}) async-start(), calls=%async_computation.2 | async-start | bytes 1622016 | tf_op jit(solution)/shard_map/all_gather | solution.py:70
  8.0 237.4 %reduce-scatter.2.cloned.1.call-start = ((), (), s32[]{:S(2)}) async-start(), calls=%async_computation.3 | async-start | bytes 2211840 | tf_op jit(solution)/shard_map/reduce_scatter | solution.py:75
  123.7 1.7 copy-start.21
  126.1 14.2 %copy-start = (f32[512,192,5]{0,1,2:T(8,128)}, f32[512,192,5]{0,1,2:T(8,128)S(1)}, u32[]{:S(2)}) copy-start(f32[512,192,5]{0,1,2:T(8,128)S(1)} %get-tuple-element.57) | copy-start | bytes 5898244
  126.8 12.1 %copy-start.2 = (f32[512,192,5]{0,1,2:T(8,128)}, f32[512,192,5]{0,1,2:T(8,128)S(1)}, u32[]{:S(2)}) copy-start(f32[512,192,5]{0,1,2:T(8,128)S(1)} %get-tuple-element.59) | copy-start | bytes 5898244
  127.5 11.4 %copy-start.4 = (f32[512,192,5]{0,1,2:T(8,128)}, f32[512,192,5]{0,1,2:T(8,128)S(1)}, u32[]{:S(2)}) copy-start(f32[512,192,5]{0,1,2:T(8,128)S(1)} %get-tuple-element.61) | copy-start | bytes 5898244
  128.2 9.3 %copy-start.6 = (f32[512,192,5]{0,1,2:T(8,128)}, f32[512,192,5]{0,1,2:T(8,128)S(1)}, u32[]{:S(2)}) copy-start(f32[512,192,5]{0,1,2:T(8,128)S(1)} %get-tuple-element.63) | copy-start | bytes 5898244
  128.9 8.6 %copy-start.8 = (f32[512,192,5]{0,1,2:T(8,128)}, f32[512,192,5]{0,1,2:T(8,128)S(1)}, u32[]{:S(2)}) copy-start(f32[512,192,5]{0,1,2:T(8,128)S(1)} %get-tuple-element.65) | copy-start | bytes 5898244
  129.5 6.3 %copy-start.10 = (f32[512,192,5]{0,1,2:T(8,128)}, f32[512,192,5]{0,1,2:T(8,128)S(1)}, u32[]{:S(2)}) copy-start(f32[512,192,5]{0,1,2:T(8,128)S(1)} %get-tuple-element.67) | copy-start | bytes 5898244
  130.2 5.6 %copy-start.12 = (f32[512,192,5]{0,1,2:T(8,128)}, f32[512,192,5]{0,1,2:T(8,128)S(1)}, u32[]{:S(2)}) copy-start(f32[512,192,5]{0,1,2:T(8,128)S(1)} %get-tuple-element.69) | copy-start | bytes 5898244
  130.9 3.5 %copy-start.14 = (f32[512,192,5]{0,1,2:T(8,128)}, f32[512,192,5]{0,1,2:T(8,128)S(1)}, u32[]{:S(2)}) copy-start(f32[512,192,5]{0,1,2:T(8,128)S(1)} %get-tuple-element.71) | copy-start | bytes 5898244
  131.6 2.8 %copy-start.16 = (f32[512,192,5]{0,1,2:T(8,128)}, f32[512,192,5]{0,1,2:T(8,128)S(1)}, u32[]{:S(2)}) copy-start(f32[512,192,5]{0,1,2:T(8,128)S(1)} %get-tuple-element.73) | copy-start | bytes 5898244
  132.3 2.1 copy-start.18
  141.7 2.5 copy-start.19
  141.7 2.6 %copy-start.22 = (bf16[6144,128]{1,0:T(8,128)(2,1)S(1)}, bf16[6144,128]{1,0:T(8,128)(2,1)}, u32[]{:S(2)}) copy-start(bf16[6144,128]{1,0:T(8,128)(2,1)} %all-gather.5.cloned.1.call-done) | copy-start | bytes 4718596
  144.4 1.5 copy-start.17
  145.9 1.5 copy-start.15
  147.4 1.5 copy-start.13
  149.0 1.5 copy-start.11
  150.5 1.5 copy-start.9
  152.1 1.5 copy-start.7
  153.6 1.5 copy-start.5
  155.2 1.5 copy-start.3
  (2 other events, 3.0 us)
Sparse Core Ops, SparseCore 0:
  9.2 66.5 all-gather.2
  77.7 63.9 all-gather.4
  166.2 79.1 reduce-scatter.1
where the time goes:
time: 254 us; the launch traced here: 252 us
  blocking collectives  110 us (43%)
  waiting for transfers between devices  80.8 us (32%)
  matrix products  25.7 us (10%)
  between operations  14.1 us (6%)
  local copies, waits for them, and re-layouts  11 us (4%)
  other arithmetic  10 us (4%)
    unnamed x1, blocking collectives  110 us
    reduce_scatter x1, waiting for transfers between devices, shards(): lax.psum_scatter(jnp.dot(attended_values, out_weight, preferred_element_t...  79.3 us
    unnamed x50, local copies, waits for them, and re-layouts  10.8 us
    dot_general x12, matrix products, attend(): jnp.einsum('hgqk,khd->hgqd', weights.astype(jnp.bfloat16), value_block, p...  10.7 us
    dot_general x12, matrix products, attend(): jnp.einsum('qhgd,khd->hgqk', query_rows, key_block, preferred_element_typ...  9.18 us
    reduce_sum x6, other arithmetic, attend(): totals = totals * rescale + jnp.sum(weights, axis=-1)  8.47 us
    dot_general x1, matrix products, shards(): jnp.dot(attended_values, out_weight, preferred_element_type=jnp.float32)  5.89 us
  transfers between devices with their start and end apart: 3, of which 1 were waited for; matrix products, arithmetic and copies ran while one was open for 9% of the time, Pallas kernels for 0%

commit v1 on v0

v1 whole, which is shorter than its diff:
```python
import math

import jax
import jax.numpy as jnp
from jax import lax
from jax.experimental import pallas as pl
from jax.experimental.pallas import tpu as pltpu
from jax.sharding import PartitionSpec as P

MESH = pl.DeviceIdType.MESH
HEAD = 128
PER_KEY = 5
CH = 96
LANES = 512
SCALE = math.log2(math.e) / math.sqrt(HEAD)
LOW = -1e30

CHIPS = [
    (0, 0), (0, 1), (0, -1), (1, 0),
    (0, 2), (0, -2), (1, 1), (1, -1),
    (0, 3), (0, -3), (1, 2), (1, -2),
    (0, 4), (1, 3), (1, -3), (1, 4),
]
SLOT = {chip: 2 * j for j, chip in enumerate(CHIPS)}
GROUP = 8
ROWS = (208, 192)
SPLIT = (112, 96)
OWN = 24
HALF = 2560


def kernel(
    q_hbm, k_hbm, v_hbm, pos_ref, w_hbm, out_ref,
    q_in, w_in, early, late, q_t, high, total, acc, tri, part, gathered,
    load_sem, send_sem, recv_sem, half_sem, out_send, out_recv,
):
    blk, inner = lax.axis_index("blk"), lax.axis_index("inner")
    ylo, z, core = blk // 16, (blk // 2) % 8, blk % 2
    yhi, x = inner // 4, inner % 4
    bufs = (early, late)

    loads = [
        pltpu.make_async_copy(k_hbm.at[pl.ds(0, CH)], early.at[0, pl.ds(0, CH)], load_sem.at[0]),
        pltpu.make_async_copy(v_hbm.at[pl.ds(0, CH)], early.at[0, pl.ds(CH, CH)], load_sem.at[1]),
        pltpu.make_async_copy(k_hbm.at[pl.ds(CH, CH)], late.at[0, pl.ds(0, CH)], load_sem.at[2]),
        pltpu.make_async_copy(v_hbm.at[pl.ds(CH, CH)], late.at[0, pl.ds(CH, CH)], load_sem.at[3]),
        pltpu.make_async_copy(q_hbm, q_in, load_sem.at[4]),
        pltpu.make_async_copy(w_hbm, w_in, load_sem.at[5]),
    ]
    for load in loads:
        load.start()
    tag = pos_ref[0].astype(jnp.float32)
    early[0, pl.ds(2 * CH, 16), :] = jnp.full((16, HEAD), tag, jnp.float32).astype(jnp.bfloat16)

    def at(dy, dz, dc=0):
        y = ylo + dy - 2 * dy * ylo
        c = core + dc - 2 * dc * core
        return (y * 16 + lax.rem(z + dz + 8, 8) * 2 + c, inner)

    barrier = pltpu.get_barrier_semaphore()
    greeted = [at(0, 1), at(0, -1), at(0, 2), at(0, -2), at(1, 0), at(0, 0, 1)]
    greeted += [(blk, lax.rem(inner + d, 8)) for d in range(1, 8)]
    for device in greeted:
        pl.semaphore_signal(barrier, inc=1, device_id=device, device_id_type=MESH)

    sends = []

    def send(phase, src, dst, device, rows=None, half=False):
        count = sum(1 for p, _ in sends if p == phase)
        lo, size = rows or (0, ROWS[phase])
        buf = bufs[phase]
        copy = pltpu.make_async_remote_copy(
            src_ref=buf.at[src, pl.ds(lo, size)],
            dst_ref=buf.at[dst, pl.ds(lo, size)],
            send_sem=send_sem.at[phase, count],
            recv_sem=half_sem.at[phase] if half else recv_sem.at[phase, dst],
            device_id=device,
            device_id_type=MESH,
        )
        copy.start()
        sends.append((phase, copy))

    def arrived(phase, slot, rows=None, half=False):
        lo, size = rows or (0, ROWS[phase])
        ref = bufs[phase].at[slot, pl.ds(lo, size)]
        sem = half_sem.at[phase] if half else recv_sem.at[phase, slot]
        pltpu.make_async_copy(ref, ref, sem).wait()

    def halves(phase):
        return (0, SPLIT[phase]), (SPLIT[phase], ROWS[phase] - SPLIT[phase])

    def sibling(phase, chip):
        send(phase, SLOT[chip], SLOT[chip] + 1, at(0, 0, 1))

    def partner(phase, dz):
        send(phase, SLOT[0, dz], SLOT[1, dz], at(1, 0))

    def stage_one(phase):
        for d in (2, -2, 1, -1):
            send(phase, 0, SLOT[0, -d], at(0, d))
        partner(phase, 0)
        sibling(phase, (0, 0))

    def stage_two(phase):
        for d in (1, -1):
            arrived(phase, SLOT[0, d])
            partner(phase, d)
            sibling(phase, (0, d))
        first, second = halves(phase)
        for d in (2, -2):
            s = d // 2
            arrived(phase, SLOT[0, d])
            send(phase, SLOT[0, d], SLOT[0, 3 * s], at(0, -s))
            send(phase, SLOT[0, d], SLOT[0, 4], at(0, -d), first if s > 0 else second, half=s < 0)
            partner(phase, d)
            sibling(phase, (0, d))
        arrived(phase, SLOT[1, 0])
        sibling(phase, (1, 0))

    def stage_three(phase):
        for d in (1, -1, 2, -2):
            arrived(phase, SLOT[1, d])
            sibling(phase, (1, d))
        for d in (3, -3):
            arrived(phase, SLOT[0, d])
            partner(phase, d)
            sibling(phase, (0, d))
        first, second = halves(phase)
        arrived(phase, SLOT[0, 4], first)
        arrived(phase, SLOT[0, 4], second, half=True)
        partner(phase, 4)
        sibling(phase, (0, 4))

    def stage_four(phase):
        for d in (3, -3, 4):
            arrived(phase, SLOT[1, d])
            sibling(phase, (1, d))

    def from_sibling(phase, group):
        for j in range(4 * group, 4 * group + 4):
            arrived(phase, 2 * j + 1)

    def attend(phase, which, group, first=False):
        buf = bufs[which]
        base = group * GROUP
        keys = buf[pl.ds(base, GROUP), pl.ds(0, CH), :].reshape(GROUP * CH, HEAD)
        values = buf[pl.ds(base, GROUP), pl.ds(CH, CH), :].reshape(GROUP * CH, HEAD)
        scores = jnp.dot(keys, q_t[phase], preferred_element_type=jnp.float32)
        if phase == which:
            tags = early[pl.ds(base, GROUP), pl.ds(2 * CH, 16), :].astype(jnp.float32)[:, :1, :]
            seen = tags < tag if phase == 0 else tags > tag
            bias = jnp.where(seen, 0.0, LOW)
            bias = jnp.concatenate([bias] * (LANES // HEAD), axis=2)
            scores = scores.reshape(GROUP, CH, LANES)
            if first:
                scores = jnp.concatenate([scores[:1] + tri[...][None], scores[1:] + bias[1:]], axis=0)
            else:
                scores = scores + bias
            scores = scores.reshape(GROUP * CH, LANES)
        old = high[phase]
        new = jnp.maximum(old, jnp.max(scores, axis=0, keepdims=True) * SCALE)
        weights = jnp.exp2(scores * SCALE - new)
        keep = jnp.exp2(old - new)
        high[phase] = new
        total[phase] = total[phase] * keep + jnp.sum(weights, axis=0, keepdims=True)
        mixed = lax.dot_general(
            values, weights.astype(jnp.bfloat16), (((0,), (0,)), ((), ())),
            preferred_element_type=jnp.float32,
        )
        acc[phase] = acc[phase] * keep + mixed

    def attend_many(phase, which, lo, hi):
        def body(group, carry):
            attend(phase, which, group)
            return carry

        lax.fori_loop(lo, hi, body, 0)

    def project(phase):
        rows = jnp.transpose(acc[phase] * (1.0 / total[phase])).astype(jnp.bfloat16)
        rows = jnp.concatenate([rows[h * CH : (h + 1) * CH] for h in range(PER_KEY)], axis=1)

        def body(j, carry):
            lo = pl.multiple_of(j * 512, 512)
            left, right = [
                jnp.dot(
                    rows, w_in[:, pl.ds(pl.multiple_of(side * HALF + lo, 512), 512)],
                    preferred_element_type=jnp.float32,
                )
                for side in range(2)
            ]
            for d in range(4):
                cut = slice(OWN * d, OWN * (d + 1))
                both = jnp.concatenate([left[cut], right[cut]], axis=0)
                part[phase, d, :, pl.ds(lo, 512)] = both.astype(jnp.bfloat16)
            return carry

        lax.fori_loop(0, HALF // 512, body, 0)

    def share(phase, d):
        to = lax.rem(x + d, 4)
        other = yhi if phase == 0 else 1 - yhi
        return other, pltpu.make_async_remote_copy(
            src_ref=part.at[phase, to],
            dst_ref=gathered.at[other * 4 + (4 - d) % 4],
            send_sem=out_send.at[phase, d],
            recv_sem=out_recv.at[other * 4 + (4 - d) % 4],
            device_id=(blk, phase * 4 + to),
            device_id_type=MESH,
        )

    def scatter(phase, wait=False):
        for d in (2, 1, 3, 0):
            other, copy = share(phase, d)
            act = copy.wait_send if wait else copy.start
            if d:
                act()
            else:
                pl.when(other == 1)(act)

    lane = lax.broadcasted_iota(jnp.int32, (CH, LANES), 1)
    start = sum(jnp.where(lane >= CH * h, CH, 0) for h in range(1, PER_KEY + 1))
    row = lax.broadcasted_iota(jnp.int32, (CH, LANES), 0)
    tri[...] = jnp.where(row <= lane - start, 0.0, LOW)
    high[...] = jnp.full(high.shape, LOW, jnp.float32)
    total[...] = jnp.zeros(total.shape, jnp.float32)
    acc[...] = jnp.zeros(acc.shape, jnp.float32)

    pl.semaphore_wait(barrier, len(greeted))
    loads[0].wait()
    loads[1].wait()
    stage_one(0)
    loads[2].wait()
    loads[3].wait()
    stage_one(1)
    loads[4].wait()
    for phase in range(2):
        heads = [q_in[pl.ds(CH * phase, CH), pl.ds(HEAD * h, HEAD)] for h in range(PER_KEY)]
        pad = jnp.zeros((LANES - PER_KEY * CH, HEAD), jnp.bfloat16)
        q_t[phase] = jnp.transpose(jnp.concatenate(heads + [pad], axis=0))

    stage_two(0)
    stage_two(1)
    from_sibling(0, 0)
    attend(0, 0, 0, first=True)
    stage_three(0)
    from_sibling(0, 1)
    attend(0, 0, 1)
    stage_three(1)
    from_sibling(0, 2)
    attend(0, 0, 2)
    stage_four(0)
    from_sibling(0, 3)
    attend(0, 0, 3)
    loads[5].wait()
    project(0)
    scatter(0)
    stage_four(1)
    attend_many(1, 0, 0, 4)
    from_sibling(1, 0)
    attend(1, 1, 0, first=True)
    for group in range(1, 4):
        from_sibling(1, group)
    attend_many(1, 1, 1, 4)
    project(1)
    scatter(1)

    for _, copy in sends:
        copy.wait_send()
    scatter(0, wait=True)
    for s in range(1, 8):
        pltpu.make_async_copy(gathered.at[s], gathered.at[s], out_recv.at[s]).wait()

    def add_up(j, carry):
        cols = pl.ds(pl.multiple_of(j * 256, 256), 256)
        summed = part[yhi, x, :, cols].astype(jnp.float32)
        for s in range(1, 8):
            summed = summed + gathered[s, :, cols].astype(jnp.float32)
        summed = summed.astype(out_ref.dtype)
        out_ref[:, cols] = summed[:OWN]
        out_ref[:, pl.ds(pl.multiple_of(HALF + j * 256, 256), 256)] = summed[OWN:]
        return carry

    lax.fori_loop(0, HALF // 256, add_up, 0)
    scatter(1, wait=True)


def shards(queries, keys, values, positions, out_weight):
    any_space = pl.BlockSpec(memory_space=pl.ANY)
    return pl.pallas_call(
        kernel,
        out_shape=jax.ShapeDtypeStruct((OWN, 2 * HALF), jnp.bfloat16),
        in_specs=[any_space] * 3 + [pl.BlockSpec(memory_space=pltpu.SMEM), any_space],
        out_specs=pl.BlockSpec(memory_space=pltpu.VMEM),
        scratch_shapes=[
            pltpu.VMEM((2 * CH, PER_KEY * HEAD), jnp.bfloat16),
            pltpu.VMEM((PER_KEY * HEAD, 2 * HALF), jnp.bfloat16),
            pltpu.VMEM((32, ROWS[0], HEAD), jnp.bfloat16),
            pltpu.VMEM((32, ROWS[1], HEAD), jnp.bfloat16),
            pltpu.VMEM((2, HEAD, LANES), jnp.bfloat16),
            pltpu.VMEM((2, 1, LANES), jnp.float32),
            pltpu.VMEM((2, 1, LANES), jnp.float32),
            pltpu.VMEM((2, HEAD, LANES), jnp.float32),
            pltpu.VMEM((CH, LANES), jnp.float32),
            pltpu.VMEM((2, 4, 2 * OWN, HALF), jnp.bfloat16),
            pltpu.VMEM((8, 2 * OWN, HALF), jnp.bfloat16),
            pltpu.SemaphoreType.DMA((6,)),
            pltpu.SemaphoreType.DMA((2, 32)),
            pltpu.SemaphoreType.DMA((2, 32)),
            pltpu.SemaphoreType.DMA((2,)),
            pltpu.SemaphoreType.DMA((2, 4)),
            pltpu.SemaphoreType.DMA((8,)),
        ],
        compiler_params=pltpu.CompilerParams(
            collective_id=0, has_side_effects=True, vmem_limit_bytes=48 << 20
        ),
        cost_estimate=pl.CostEstimate(
            flops=4_000_000_000, bytes_accessed=10_000_000, transcendentals=5_000_000
        ),
    )(queries, keys, values, positions, out_weight)


def solution(mesh):
    placed = (P("blk", "inner"), P("blk", "inner"), P("blk", "inner"), P("blk"), P("inner", None))
    return jax.shard_map(
        shards, mesh=mesh, in_specs=placed, out_specs=P(("blk", "inner"), None), check_vma=False
    )
```

time: 254 us -> 70.9 us (0.28)
  blocking collectives: 110 us -> 0 us
  waiting for transfers between devices: 80.8 us -> 0 us
  Pallas kernels: 0 us -> 66.3 us
  matrix products: 25.7 us -> 0 us
  between operations: 14.1 us -> 0.01 us
  other arithmetic: 10 us -> 0 us
  local copies, waits for them, and re-layouts: 11 us -> 3.91 us
    unnamed x1 -> x0, blocking collectives: 110 us -> none
    reduce_scatter x1 -> x0, waiting for transfers between devices: 79.3 us -> none  [shards(): lax.psum_scatter(jnp.dot(attended_values, out_weight, preferred_element_t...]
    pallas_call x0 -> x1, Pallas kernels: none -> 66.3 us  [shards(): pl.pallas_call(kernel, out_shape=jax.ShapeDtypeStruct((OWN, 2 * HALF), jn...]
    dot_general x25 -> x0, matrix products: 25.7 us -> none  [the longest x12 10.7 us: attend(): jnp.einsum('hgqk,khd->hgqd', weights.astype(jnp.bfloat16), value_block, p...]
    reduce_sum x6 -> x0, other arithmetic: 8.47 us -> none  [attend(): totals = totals * rescale + jnp.sum(weights, axis=-1)]
    unnamed x50 -> x9, local copies, waits for them, and re-layouts: 10.8 us -> 3.91 us
  transfers between devices with their start and end apart: 3 -> 0, of which waited for: 1 -> 0; matrix products, arithmetic and copies ran while one was open for 9% -> 0% of each run, Pallas kernels for 0% -> 0%
where the time goes in v1:
time: 70.9 us; the launch traced here: 70.2 us
  Pallas kernels  66.3 us (94%)
  local copies, waits for them, and re-layouts  3.91 us (6%)
    pallas_call x1, Pallas kernels, shards(): pl.pallas_call(kernel, out_shape=jax.ShapeDtypeStruct((OWN, 2 * HALF), jn...  66.3 us
    unnamed x9, local copies, waits for them, and re-layouts  3.91 us

profile of v1, /device:TPU:24, one launch (start us, length us, event | category | flops | bytes accessed | tf_op | source)
XLA Modules:
  0.0 70.2 jit_solution(11573946910378738979)
XLA Ops:
  0.0 0.0 copy-start
  0.0 0.9 %copy-done = bf16[192,640]{1,0:T(8,128)(2,1)S(1)} copy-done((bf16[192,640]{1,0:T(8,128)(2,1)S(1)}, bf16[192,640]{1,0:T(8,128)(2,1)}, u32[]{:S(2)}) %copy-start) | copy-done | bytes 245784
  0.9 0.0 copy-start.1
  0.9 0.8 %copy-done.1 = bf16[192,128]{1,0:T(8,128)(2,1)S(1)} copy-done((bf16[192,128]{1,0:T(8,128)(2,1)S(1)}, bf16[192,128]{1,0:T(8,128)(2,1)}, u32[]{:S(2)}) %copy-start.1) | copy-done | bytes 49176
  1.7 0.0 copy-start.2
  1.7 0.8 %copy-done.2 = bf16[192,128]{1,0:T(8,128)(2,1)S(1)} copy-done((bf16[192,128]{1,0:T(8,128)(2,1)S(1)}, bf16[192,128]{1,0:T(8,128)(2,1)}, u32[]{:S(2)}) %copy-start.2) | copy-done | bytes 49176
  2.5 0.0 copy-start.3
  2.5 0.7 copy-done.3
  3.2 66.3 %shard_map.55 = bf16[24,5120]{1,0:T(8,128)(2,1)S(1)} custom-call(bf16[192,640]{1,0:T(8,128)(2,1)S(1)} %copy-done, bf16[192,128]{1,0:T(8,128)(2,1)S(1)} %copy-done.1, bf16[192,128]{1,0:T(8,128)(2,1)S(1)} %copy-done.2, s32[192]{0:T(256)S(1)} %copy-done.3, bf16[640,5120]{1,0:T(8,128)(2,1)} %w_hbm.1), custom_call_target="tpu_custom_call" | custom-call | flops 4000000000 | bytes 10000000 | tf_op jit(solution)/shard_map/pallas_call | solution.py:290
  69.5 0.7 copy.7
Async XLA Ops:
  0.0 0.9 %copy-start = (bf16[192,640]{1,0:T(8,128)(2,1)S(1)}, bf16[192,640]{1,0:T(8,128)(2,1)}, u32[]{:S(2)}) copy-start(bf16[192,640]{1,0:T(8,128)(2,1)} %q_hbm.1) | copy-start | bytes 737284
  0.9 0.8 %copy-start.1 = (bf16[192,128]{1,0:T(8,128)(2,1)S(1)}, bf16[192,128]{1,0:T(8,128)(2,1)}, u32[]{:S(2)}) copy-start(bf16[192,128]{1,0:T(8,128)(2,1)} %k_hbm.1) | copy-start | bytes 147460
  1.7 0.8 %copy-start.2 = (bf16[192,128]{1,0:T(8,128)(2,1)S(1)}, bf16[192,128]{1,0:T(8,128)(2,1)}, u32[]{:S(2)}) copy-start(bf16[192,128]{1,0:T(8,128)(2,1)} %v_hbm.1) | copy-start | bytes 147460
  2.5 0.7 copy-start.3

commit v2 on v1

v2 whole, which is shorter than its diff:
```python
import math

import jax
import jax.numpy as jnp
from jax import lax
from jax.experimental import pallas as pl
from jax.experimental.pallas import tpu as pltpu
from jax.sharding import PartitionSpec as P

MESH = pl.DeviceIdType.MESH
HEAD = 128
PER_KEY = 5
CH = 96
LANES = 512
SCALE = math.log2(math.e) / math.sqrt(HEAD)
LOW = -1e30

CHIPS = [
    (0, 0), (0, 1), (0, -1), (1, 0),
    (0, 2), (0, -2), (1, 1), (1, -1),
    (0, 3), (0, -3), (1, 2), (1, -2),
    (0, 4), (1, 3), (1, -3), (1, 4),
]
SLOT = {chip: 2 * j for j, chip in enumerate(CHIPS)}
GROUP = 8
ROWS = (208, 192)
OWN = 24
HALF = 2560
CHUNKS = 4
WIDE = HALF // CHUNKS


TREES = (
    {
        (0, 0): [(0, 2), (0, -2), (0, 1), (0, -1), (1, 0)],
        (0, 1): [(1, 1)],
        (0, -1): [(1, -1)],
        (0, 2): [(0, 3), (0, 4), (1, 2)],
        (0, -2): [(0, -3), (1, -2)],
        (1, 2): [(1, 3)],
        (1, -2): [(1, -3), (1, 4)],
    },
    {
        (0, 0): [(0, 1), (0, -1), (1, 0)],
        (0, 1): [(0, 2), (1, 1)],
        (0, -1): [(0, -2), (1, -1)],
        (0, 2): [(0, 3), (1, 2)],
        (0, -2): [(0, -3), (1, -2)],
        (0, 3): [(0, 4)],
        (1, 2): [(1, 3)],
        (1, -2): [(1, -3)],
        (1, -3): [(1, 4)],
    },
)


def slot_of(chip):
    dy, dz = chip
    return SLOT[dy, dz if dz == 4 else -dz]


def kernel(
    q_hbm, k_hbm, v_hbm, pos_hbm, w_hbm, out_ref,
    q_in, w_in, pos_in, early, late, q_t, high, total, acc, tri,
    part, through, passed, beside, across, crossed,
    load_sem, send_sem, recv_sem, row_send, row_recv,
):
    blk, inner = lax.axis_index("blk"), lax.axis_index("inner")
    ylo, z, core = blk // 16, (blk // 2) % 8, blk % 2
    yhi, x = inner // 4, inner % 4
    bufs = (early, late)

    loads = [
        pltpu.make_async_copy(pos_hbm, pos_in, load_sem.at[6]),
        pltpu.make_async_copy(k_hbm.at[pl.ds(0, CH)], early.at[0, pl.ds(0, CH)], load_sem.at[0]),
        pltpu.make_async_copy(v_hbm.at[pl.ds(0, CH)], early.at[0, pl.ds(CH, CH)], load_sem.at[1]),
        pltpu.make_async_copy(k_hbm.at[pl.ds(CH, CH)], late.at[0, pl.ds(0, CH)], load_sem.at[2]),
        pltpu.make_async_copy(v_hbm.at[pl.ds(CH, CH)], late.at[0, pl.ds(CH, CH)], load_sem.at[3]),
        pltpu.make_async_copy(q_hbm, q_in, load_sem.at[4]),
        pltpu.make_async_copy(w_hbm, w_in, load_sem.at[5]),
    ]
    for load in loads:
        load.start()

    def at(dy, dz, dc=0):
        y = ylo + dy - 2 * dy * ylo
        c = core + dc - 2 * dc * core
        return (y * 16 + lax.rem(z + dz + 8, 8) * 2 + c, inner)

    def along(d):
        return (blk, yhi * 4 + lax.rem(x + d + 4, 4))

    opposite = (blk, lax.rem(inner + 4, 8))
    barrier = pltpu.get_barrier_semaphore()
    greeted = [at(0, 1), at(0, -1), at(0, 2), at(0, -2), at(1, 0), at(0, 0, 1)]
    greeted += [along(1), along(-1), opposite]
    for device in greeted:
        pl.semaphore_signal(barrier, inc=1, device_id=device, device_id_type=MESH)

    sends = []

    def send(phase, src, dst, device):
        count = sum(1 for p, _ in sends if p == phase)
        copy = pltpu.make_async_remote_copy(
            src_ref=bufs[phase].at[src],
            dst_ref=bufs[phase].at[dst],
            send_sem=send_sem.at[phase, count],
            recv_sem=recv_sem.at[phase, dst],
            device_id=device,
            device_id_type=MESH,
        )
        copy.start()
        sends.append((phase, copy))

    def arrived(phase, slot):
        ref = bufs[phase].at[slot]
        pltpu.make_async_copy(ref, ref, recv_sem.at[phase, slot]).wait()

    def pass_on(phase, *chips):
        for chip in chips:
            slot = slot_of(chip)
            if chip != (0, 0):
                arrived(phase, slot)
            for to in TREES[phase].get(chip, ()):
                dz = (to[1] - chip[1] + 4) % 8 - 4
                send(phase, slot, slot_of(to), at(to[0] - chip[0], dz))
            send(phase, slot, slot + 1, at(0, 0, 1))

    def from_sibling(phase, group):
        for j in range(4 * group, 4 * group + 4):
            arrived(phase, 2 * j + 1)

    def attend(phase, which, group, first=False):
        buf = bufs[which]
        base = group * GROUP
        keys = buf[pl.ds(base, GROUP), pl.ds(0, CH), :].reshape(GROUP * CH, HEAD)
        values = buf[pl.ds(base, GROUP), pl.ds(CH, CH), :].reshape(GROUP * CH, HEAD)
        scores = jnp.dot(keys, q_t[phase], preferred_element_type=jnp.float32)
        if phase == which:
            tags = early[pl.ds(base, GROUP), pl.ds(2 * CH, 16), :].astype(jnp.float32)[:, :1, :]
            seen = tags < tag if phase == 0 else tags > tag
            bias = jnp.where(seen, 0.0, LOW)
            bias = jnp.concatenate([bias] * (LANES // HEAD), axis=2)
            scores = scores.reshape(GROUP, CH, LANES)
            if first:
                scores = jnp.concatenate([scores[:1] + tri[...][None], scores[1:] + bias[1:]], axis=0)
            else:
                scores = scores + bias
            scores = scores.reshape(GROUP * CH, LANES)
        old = high[phase]
        new = jnp.maximum(old, jnp.max(scores, axis=0, keepdims=True) * SCALE)
        weights = jnp.exp2(scores * SCALE - new)
        keep = jnp.exp2(old - new)
        high[phase] = new
        total[phase] = total[phase] * keep + jnp.sum(weights, axis=0, keepdims=True)
        mixed = lax.dot_general(
            values, weights.astype(jnp.bfloat16), (((0,), (0,)), ((), ())),
            preferred_element_type=jnp.float32,
        )
        acc[phase] = acc[phase] * keep + mixed

    def attend_many(phase, which, lo, hi):
        def body(group, carry):
            attend(phase, which, group)
            return carry

        lax.fori_loop(lo, hi, body, 0)

    row_sends = []

    def row_send_to(kind, phase, j, src, dst, device):
        copy = pltpu.make_async_remote_copy(
            src_ref=src, dst_ref=dst.at[phase, j],
            send_sem=row_send.at[kind, phase, j], recv_sem=row_recv.at[kind, phase, j],
            device_id=device, device_id_type=MESH,
        )
        return copy

    def row_wait(kind, phase, j, dst):
        ref = dst.at[phase, j]
        pltpu.make_async_copy(ref, ref, row_recv.at[kind, phase, j]).wait()

    def way(j):
        return 1 if j % 2 == 0 else -1

    def project(phase):
        rows = jnp.transpose(acc[phase] * (1.0 / total[phase])).astype(jnp.bfloat16)
        rows = jnp.concatenate([rows[h * CH : (h + 1) * CH] for h in range(PER_KEY)], axis=1)
        for piece in range(CHUNKS // 2):
            left, right = [
                jnp.dot(
                    rows, w_in[:, side * HALF + piece * 2 * WIDE : side * HALF + (piece + 1) * 2 * WIDE],
                    preferred_element_type=jnp.float32,
                )
                for side in range(2)
            ]
            for j in (2 * piece, 2 * piece + 1):
                cols = slice((j % 2) * WIDE, (j % 2 + 1) * WIDE)
                for d in range(4):
                    cut = slice(OWN * d, OWN * (d + 1))
                    both = jnp.concatenate([left[cut, cols], right[cut, cols]], axis=0)
                    part[phase, j, d] = both.astype(jnp.bfloat16)
            for j in (2 * piece, 2 * piece + 1):
                s = way(j)
                copy = row_send_to(0, phase, j, part.at[phase, j, lax.rem(x + 2, 4)], through, along(s))
                copy.start()
                row_sends.append(copy)
            for j in (2 * piece, 2 * piece + 1):
                s = way(j)
                copy = row_send_to(1, phase, j, part.at[phase, j, lax.rem(x + 4 - s, 4)], beside, along(-s))
                copy.start()
                row_sends.append(copy)

    def go_through(phase, *chunks):
        for j in chunks:
            s = way(j)
            row_wait(0, phase, j, through)
            mine = part[phase, j, lax.rem(x + 4 + s, 4)].astype(jnp.float32)
            through[phase, j] = (mine + through[phase, j].astype(jnp.float32)).astype(jnp.bfloat16)
            copy = row_send_to(2, phase, j, through.at[phase, j], passed, along(s))
            copy.start()
            row_sends.append(copy)

    def ring_sum(phase, j):
        row_wait(1, phase, j, beside)
        row_wait(2, phase, j, passed)
        summed = part[phase, j, x].astype(jnp.float32) + beside[phase, j].astype(jnp.float32)
        return summed + passed[phase, j].astype(jnp.float32)

    def cross_copy(phase, j):
        return row_send_to(3, phase, j, across.at[phase, j], crossed, opposite)

    def cross(phase, *chunks):
        @pl.when(yhi != phase)
        def _():
            for j in chunks:
                across[phase, j] = ring_sum(phase, j).astype(jnp.bfloat16)
                cross_copy(phase, j).start()

    def finish(phase):
        @pl.when(yhi == phase)
        def _():
            for j in range(CHUNKS):
                summed = ring_sum(phase, j)
                row_wait(3, phase, j, crossed)
                summed = (summed + crossed[phase, j].astype(jnp.float32)).astype(out_ref.dtype)
                out_ref[:, j * WIDE : (j + 1) * WIDE] = summed[:OWN]
                out_ref[:, HALF + j * WIDE : HALF + (j + 1) * WIDE] = summed[OWN:]

        @pl.when(yhi != phase)
        def _():
            for j in range(CHUNKS):
                cross_copy(phase, j).wait_send()

    lane = lax.broadcasted_iota(jnp.int32, (CH, LANES), 1)
    start = sum(jnp.where(lane >= CH * h, CH, 0) for h in range(1, PER_KEY + 1))
    row = lax.broadcasted_iota(jnp.int32, (CH, LANES), 0)
    tri[...] = jnp.where(row <= lane - start, 0.0, LOW)
    high[...] = jnp.full(high.shape, LOW, jnp.float32)
    total[...] = jnp.zeros(total.shape, jnp.float32)
    acc[...] = jnp.zeros(acc.shape, jnp.float32)

    pl.semaphore_wait(barrier, len(greeted))
    loads[0].wait()
    tag = pos_in[0].astype(jnp.float32)
    early[0, pl.ds(2 * CH, 16), :] = jnp.full((16, HEAD), tag, jnp.float32).astype(jnp.bfloat16)
    loads[1].wait()
    loads[2].wait()
    pass_on(0, (0, 0))
    loads[3].wait()
    loads[4].wait()
    pass_on(1, (0, 0))
    loads[5].wait()
    for phase in range(2):
        heads = [q_in[pl.ds(CH * phase, CH), pl.ds(HEAD * h, HEAD)] for h in range(PER_KEY)]
        pad = jnp.zeros((LANES - PER_KEY * CH, HEAD), jnp.bfloat16)
        q_t[phase] = jnp.transpose(jnp.concatenate(heads + [pad], axis=0))

    pass_on(0, (0, 2), (0, -2), (0, 1), (0, -1), (1, 0))
    pass_on(1, (0, 1), (0, -1), (1, 0))
    from_sibling(0, 0)
    attend(0, 0, 0, first=True)
    attend(1, 0, 0)
    pass_on(0, (1, 2), (1, -2), (1, 1), (1, -1))
    pass_on(1, (0, 2), (0, -2))
    from_sibling(0, 1)
    attend(0, 0, 1)
    pass_on(0, (0, 3), (0, -3), (0, 4))
    attend(1, 0, 1)
    pass_on(1, (1, 1), (1, -1))
    from_sibling(0, 2)
    attend(0, 0, 2)
    pass_on(1, (0, 3), (0, -3))
    pass_on(0, (1, 3), (1, -3), (1, 4))
    from_sibling(0, 3)
    attend(0, 0, 3)
    loads[6].wait()
    project(0)
    pass_on(1, (1, 2), (1, -2), (0, 4))
    attend(1, 0, 2)
    attend(1, 0, 3)
    pass_on(1, (1, 3), (1, -3))
    from_sibling(1, 0)
    attend(1, 1, 0, first=True)
    pass_on(1, (1, 4))
    go_through(0, 0, 1)
    from_sibling(1, 1)
    attend(1, 1, 1)
    go_through(0, 2, 3)
    for group in range(2, 4):
        from_sibling(1, group)
        attend(1, 1, group)
    project(1)
    cross(0, *range(CHUNKS))
    go_through(1, *range(CHUNKS))
    finish(0)
    cross(1, *range(CHUNKS))
    finish(1)
    for _, copy in sends:
        copy.wait_send()
    for copy in row_sends:
        copy.wait_send()


def shards(queries, keys, values, positions, out_weight):
    any_space = pl.BlockSpec(memory_space=pl.ANY)
    return pl.pallas_call(
        kernel,
        out_shape=jax.ShapeDtypeStruct((OWN, 2 * HALF), jnp.bfloat16),
        in_specs=[any_space] * 5,
        out_specs=pl.BlockSpec(memory_space=pltpu.VMEM),
        scratch_shapes=[
            pltpu.VMEM((2 * CH, PER_KEY * HEAD), jnp.bfloat16),
            pltpu.VMEM((PER_KEY * HEAD, 2 * HALF), jnp.bfloat16),
            pltpu.SMEM((2 * CH,), jnp.int32),
            pltpu.VMEM((32, ROWS[0], HEAD), jnp.bfloat16),
            pltpu.VMEM((32, ROWS[1], HEAD), jnp.bfloat16),
            pltpu.VMEM((2, HEAD, LANES), jnp.bfloat16),
            pltpu.VMEM((2, 1, LANES), jnp.float32),
            pltpu.VMEM((2, 1, LANES), jnp.float32),
            pltpu.VMEM((2, HEAD, LANES), jnp.float32),
            pltpu.VMEM((CH, LANES), jnp.float32),
            pltpu.VMEM((2, CHUNKS, 4, 2 * OWN, WIDE), jnp.bfloat16),
            *[pltpu.VMEM((2, CHUNKS, 2 * OWN, WIDE), jnp.bfloat16) for _ in range(5)],
            pltpu.SemaphoreType.DMA((7,)),
            pltpu.SemaphoreType.DMA((2, 32)),
            pltpu.SemaphoreType.DMA((2, 32)),
            pltpu.SemaphoreType.DMA((4, 2, CHUNKS)),
            pltpu.SemaphoreType.DMA((4, 2, CHUNKS)),
        ],
        compiler_params=pltpu.CompilerParams(
            collective_id=0, has_side_effects=True, vmem_limit_bytes=62 << 20
        ),
        cost_estimate=pl.CostEstimate(
            flops=4_000_000_000, bytes_accessed=10_000_000, transcendentals=5_000_000
        ),
    )(queries, keys, values, positions, out_weight)


def solution(mesh):
    placed = (P("blk", "inner"), P("blk", "inner"), P("blk", "inner"), P("blk"), P("inner", None))
    return jax.shard_map(
        shards, mesh=mesh, in_specs=placed, out_specs=P(("blk", "inner"), None), check_vma=False
    )
```

time: 70.9 us -> 55.6 us (0.78)
  Pallas kernels: 66.3 us -> 53.7 us
  local copies, waits for them, and re-layouts: 3.91 us -> 1.65 us
    pallas_call x1, Pallas kernels: 66.3 us -> 53.7 us  [shards(): pl.pallas_call(kernel, out_shape=jax.ShapeDtypeStruct((OWN, 2 * HALF), jn...]
    unnamed x9 -> x1, local copies, waits for them, and re-layouts: 3.91 us -> 1.65 us
where the time goes in v2:
time: 55.6 us; the launch traced here: 55.3 us
  Pallas kernels  53.7 us (97%)
  local copies, waits for them, and re-layouts  1.65 us (3%)
    pallas_call x1, Pallas kernels, shards(): pl.pallas_call(kernel, out_shape=jax.ShapeDtypeStruct((OWN, 2 * HALF), jn...  53.7 us
    unnamed x1, local copies, waits for them, and re-layouts  1.65 us

profile of v2, /device:TPU:24, one launch (start us, length us, event | category | flops | bytes accessed | tf_op | source)
XLA Modules:
  0.0 55.3 jit_solution(1936917770859205044)
XLA Ops:
  0.0 53.7 %shard_map.55 = bf16[24,5120]{1,0:T(8,128)(2,1)} custom-call(bf16[192,640]{1,0:T(8,128)(2,1)} %q_hbm.1, bf16[192,128]{1,0:T(8,128)(2,1)} %k_hbm.1, bf16[192,128]{1,0:T(8,128)(2,1)} %v_hbm.1, s32[192]{0:T(256)} %pos_hbm.1, bf16[640,5120]{1,0:T(8,128)(2,1)} %w_hbm.1), custom_call_target="tpu_custom_call" | custom-call | flops 4000000000 | bytes 10000000 | tf_op jit(solution)/shard_map/pallas_call | solution.py:327
  53.7 1.7 %copy.7 = bf16[24,5120]{1,0:T(8,128)(2,1)} copy(bf16[24,5120]{1,0:T(8,128)(2,1)} %shard_map.55) | data formatting | bytes 491520

commit v3 on v2

--- a/solution.py
+++ b/solution.py
@@ -15,48 +15,78 @@
 SCALE = math.log2(math.e) / math.sqrt(HEAD)
 LOW = -1e30
 
-CHIPS = [
-    (0, 0), (0, 1), (0, -1), (1, 0),
-    (0, 2), (0, -2), (1, 1), (1, -1),
-    (0, 3), (0, -3), (1, 2), (1, -2),
-    (0, 4), (1, 3), (1, -3), (1, 4),
+CHIPS = (
+    [(0, 0), (0, -1), (1, 0), (0, 2), (0, -2), (1, -1), (1, 1), (0, 3), (1, 2), (1, -3), (1, -2), (0, -3), (0, 1), (0, 4), (1, 4), (1, 3)],
+    [(0, 0), (0, -1), (1, 0), (0, 2), (1, -1), (0, 3), (1, -2), (0, 4), (1, 3), (0, 1), (0, -2), (1, -3), (0, -3), (1, 4), (1, 1), (1, 2)],
+)
+TREES = (
+    {
+        (0, 0): [(0, -1), (0, 2), (1, 0)],
+        (0, -1): [(0, -2), (1, -1)],
+        (1, 0): [(1, 1), (1, -3)],
+        (0, 2): [(0, 3), (1, 2)],
+        (0, -2): [(0, -3), (1, -2)],
+        (1, 1): [(0, 1)],
+        (0, 3): [(0, 4), (1, 3)],
+        (1, -3): [(1, 4)],
+    },
+    {
+        (0, 0): [(0, -1), (0, 2), (1, 0)],
+        (0, -1): [(1, -1)],
+        (0, 2): [(0, 3)],
+        (1, -1): [(1, -2)],
+        (0, 3): [(0, 4), (1, 3), (0, 1)],
+        (1, -2): [(0, -2), (1, 1), (1, -3)],
+        (0, 4): [(0, -3), (1, 4)],
+        (1, 3): [(1, 2)],
+    },
+)
+PLAN = [
+    ("take", 0, (0, -1), (1, 0)),
+    ("take", 1, (0, -1), (1, 0)),
+    ("take", 0, (0, 2)),
+    ("take", 1, (0, 2)),
+    ("take", 0, (0, -2), (1, -1), (1, 1)),
+    ("attend", 0, 0, 0),
+    ("take", 1, (1, -1)),
+    ("attend", 1, 1, 0),
+    ("take", 0, (0, 3), (1, 2), (1, -3)),
+    ("attend", 1, 0, 0),
+    ("take", 1, (0, 3)),
+    ("take", 0, (1, -2), (0, -3)),
+    ("attend", 0, 0, 1),
+    ("take", 1, (1, -2)),
+    ("take", 0, (0, 1), (0, 4)),
+    ("attend", 0, 0, 2),
+    ("take", 0, (1, 4), (1, 3)),
+    ("take", 1, (0, 4)),
+    ("attend", 1, 0, 1),
+    ("take", 1, (1, 3), (0, 1)),
+    ("attend", 0, 0, 3),
+    ("take", 1, (0, -2), (1, -3)),
+    ("project", 0),
+    ("take", 1, (0, -3), (1, 4), (1, 1), (1, 2)),
+    ("attend", 1, 1, 1),
+    ("attend", 1, 1, 2),
+    ("attend", 1, 1, 3),
+    ("attend", 1, 0, 2),
+    ("through", 0, 0, 1),
+    ("attend", 1, 0, 3),
+    ("through", 0, 2, 3),
+    ("cross", 0, 0, 1, 2, 3),
+    ("project", 1),
 ]
-SLOT = {chip: 2 * j for j, chip in enumerate(CHIPS)}
+SLOT = tuple({chip: 2 * j for j, chip in enumerate(chips)} for chips in CHIPS)
 GROUP = 8
-ROWS = (208, 192)
+ROWS = (208, 208)
 OWN = 24
 HALF = 2560
 CHUNKS = 4
 WIDE = HALF // CHUNKS
 
 
-TREES = (
-    {
-        (0, 0): [(0, 2), (0, -2), (0, 1), (0, -1), (1, 0)],
-        (0, 1): [(1, 1)],
-        (0, -1): [(1, -1)],
-        (0, 2): [(0, 3), (0, 4), (1, 2)],
-        (0, -2): [(0, -3), (1, -2)],
-        (1, 2): [(1, 3)],
-        (1, -2): [(1, -3), (1, 4)],
-    },
-    {
-        (0, 0): [(0, 1), (0, -1), (1, 0)],
-        (0, 1): [(0, 2), (1, 1)],
-        (0, -1): [(0, -2), (1, -1)],
-        (0, 2): [(0, 3), (1, 2)],
-        (0, -2): [(0, -3), (1, -2)],
-        (0, 3): [(0, 4)],
-        (1, 2): [(1, 3)],
-        (1, -2): [(1, -3)],
-        (1, -3): [(1, 4)],
-    },
-)
-
-
-def slot_of(chip):
-    dy, dz = chip
-    return SLOT[dy, dz if dz == 4 else -dz]
+def step(chip, to):
+    return abs(to[0] - chip[0]), (to[1] - chip[1] + 3) % 8 - 3
 
 
 def kernel(
@@ -85,14 +115,16 @@
     def at(dy, dz, dc=0):
         y = ylo + dy - 2 * dy * ylo
         c = core + dc - 2 * dc * core
-        return (y * 16 + lax.rem(z + dz + 8, 8) * 2 + c, inner)
+        return (y * 16 + lax.rem(z + dz * (1 - 2 * core) + 8, 8) * 2 + c, inner)
 
     def along(d):
         return (blk, yhi * 4 + lax.rem(x + d + 4, 4))
 
     opposite = (blk, lax.rem(inner + 4, 8))
     barrier = pltpu.get_barrier_semaphore()
-    greeted = [at(0, 1), at(0, -1), at(0, 2), at(0, -2), at(1, 0), at(0, 0, 1)]
+    steps = {step(a, b)[1] for tree in TREES for a, ends in tree.items() for b in ends}
+    steps = sorted({d % 8 for d in steps if d} | {-d % 8 for d in steps if d})
+    greeted = [at(0, d) for d in steps] + [at(1, 0), at(0, 0, 1)]
     greeted += [along(1), along(-1), opposite]
     for device in greeted:
         pl.semaphore_signal(barrier, inc=1, device_id=device, device_id_type=MESH)
@@ -118,15 +150,19 @@
 
     def pass_on(phase, *chips):
         for chip in chips:
-            slot = slot_of(chip)
+            slot = SLOT[phase][chip]
             if chip != (0, 0):
                 arrived(phase, slot)
             for to in TREES[phase].get(chip, ()):
-                dz = (to[1] - chip[1] + 4) % 8 - 4
-                send(phase, slot, slot_of(to), at(to[0] - chip[0], dz))
+                send(phase, slot, SLOT[phase][to], at(*step(chip, to)))
             send(phase, slot, slot + 1, at(0, 0, 1))
 
-    def from_sibling(phase, group):
+    taken = set()
+
+    def from_sibling_once(phase, group):
+        if (phase, group) in taken:
+            return
+        taken.add((phase, group))
         for j in range(4 * group, 4 * group + 4):
             arrived(phase, 2 * j + 1)
 
@@ -137,7 +173,7 @@
         values = buf[pl.ds(base, GROUP), pl.ds(CH, CH), :].reshape(GROUP * CH, HEAD)
         scores = jnp.dot(keys, q_t[phase], preferred_element_type=jnp.float32)
         if phase == which:
-            tags = early[pl.ds(base, GROUP), pl.ds(2 * CH, 16), :].astype(jnp.float32)[:, :1, :]
+            tags = buf[pl.ds(base, GROUP), pl.ds(2 * CH, 16), :].astype(jnp.float32)[:, :1, :]
             seen = tags < tag if phase == 0 else tags > tag
             bias = jnp.where(seen, 0.0, LOW)
             bias = jnp.concatenate([bias] * (LANES // HEAD), axis=2)
@@ -159,13 +195,6 @@
         )
         acc[phase] = acc[phase] * keep + mixed
 
-    def attend_many(phase, which, lo, hi):
-        def body(group, carry):
-            attend(phase, which, group)
-            return carry
-
-        lax.fori_loop(lo, hi, body, 0)
-
     row_sends = []
 
     def row_send_to(kind, phase, j, src, dst, device):
@@ -184,6 +213,8 @@
         return 1 if j % 2 == 0 else -1
 
     def project(phase):
+        if phase == 0:
+            loads[6].wait()
         rows = jnp.transpose(acc[phase] * (1.0 / total[phase])).astype(jnp.bfloat16)
         rows = jnp.concatenate([rows[h * CH : (h + 1) * CH] for h in range(PER_KEY)], axis=1)
         for piece in range(CHUNKS // 2):
@@ -263,7 +294,8 @@
     pl.semaphore_wait(barrier, len(greeted))
     loads[0].wait()
     tag = pos_in[0].astype(jnp.float32)
-    early[0, pl.ds(2 * CH, 16), :] = jnp.full((16, HEAD), tag, jnp.float32).astype(jnp.bfloat16)
+    for buf in bufs:
+        buf[0, pl.ds(2 * CH, 16), :] = jnp.full((16, HEAD), tag, jnp.float32).astype(jnp.bfloat16)
     loads[1].wait()
     loads[2].wait()
     pass_on(0, (0, 0))
@@ -276,45 +308,23 @@
         pad = jnp.zeros((LANES - PER_KEY * CH, HEAD), jnp.bfloat16)
         q_t[phase] = jnp.transpose(jnp.concatenate(heads + [pad], axis=0))
 
-    pass_on(0, (0, 2), (0, -2), (0, 1), (0, -1), (1, 0))
-    pass_on(1, (0, 1), (0, -1), (1, 0))
-    from_sibling(0, 0)
-    attend(0, 0, 0, first=True)
-    attend(1, 0, 0)
-    pass_on(0, (1, 2), (1, -2), (1, 1), (1, -1))
-    pass_on(1, (0, 2), (0, -2))
-    from_sibling(0, 1)
-    attend(0, 0, 1)
-    pass_on(0, (0, 3), (0, -3), (0, 4))
-    attend(1, 0, 1)
-    pass_on(1, (1, 1), (1, -1))
-    from_sibling(0, 2)
-    attend(0, 0, 2)
-    pass_on(1, (0, 3), (0, -3))
-    pass_on(0, (1, 3), (1, -3), (1, 4))
-    from_sibling(0, 3)
-    attend(0, 0, 3)
-    loads[6].wait()
-    project(0)
-    pass_on(1, (1, 2), (1, -2), (0, 4))
-    attend(1, 0, 2)
-    attend(1, 0, 3)
-    pass_on(1, (1, 3), (1, -3))
-    from_sibling(1, 0)
-    attend(1, 1, 0, first=True)
-    pass_on(1, (1, 4))
-    go_through(0, 0, 1)
-    from_sibling(1, 1)
-    attend(1, 1, 1)
-    go_through(0, 2, 3)
-    for group in range(2, 4):
-        from_sibling(1, group)
-        attend(1, 1, group)
-    project(1)
-    cross(0, *range(CHUNKS))
-    go_through(1, *range(CHUNKS))
+    for what, *which in PLAN:
+        if what == "take":
+            pass_on(*which)
+        elif what == "attend":
+            phase, side, group = which
+            from_sibling_once(side, group)
+            attend(phase, side, group, first=phase == side and group == 0)
+        elif what == "project":
+            project(*which)
+        elif what == "cross":
+            cross(*which)
+        elif what == "through":
+            go_through(*which)
+    go_through(1, 0, 1)
+    go_through(1, 2, 3)
+    cross(1, *range(CHUNKS))
     finish(0)
-    cross(1, *range(CHUNKS))
     finish(1)
     for _, copy in sends:
         copy.wait_send()

time: 55.6 us -> 53.6 us (0.964)
  Pallas kernels: 53.7 us -> 51.8 us
    pallas_call x1, Pallas kernels: 53.7 us -> 51.8 us  [shards(): pl.pallas_call(kernel, out_shape=jax.ShapeDtypeStruct((OWN, 2 * HALF), jn...]
where the time goes in v3:
time: 53.6 us; the launch traced here: 53.5 us
  Pallas kernels  51.8 us (97%)
  local copies, waits for them, and re-layouts  1.65 us (3%)
    pallas_call x1, Pallas kernels, shards(): pl.pallas_call(kernel, out_shape=jax.ShapeDtypeStruct((OWN, 2 * HALF), jn...  51.8 us
    unnamed x1, local copies, waits for them, and re-layouts  1.65 us

profile of v3, /device:TPU:24, one launch (start us, length us, event | category | flops | bytes accessed | tf_op | source)
XLA Modules:
  0.0 53.5 jit_solution(15740427879938553861)
XLA Ops:
  0.0 51.8 %shard_map.55 = bf16[24,5120]{1,0:T(8,128)(2,1)} custom-call(bf16[192,640]{1,0:T(8,128)(2,1)} %q_hbm.1, bf16[192,128]{1,0:T(8,128)(2,1)} %k_hbm.1, bf16[192,128]{1,0:T(8,128)(2,1)} %v_hbm.1, s32[192]{0:T(256)} %pos_hbm.1, bf16[640,5120]{1,0:T(8,128)(2,1)} %w_hbm.1), custom_call_target="tpu_custom_call" | custom-call | flops 4000000000 | bytes 10000000 | tf_op jit(solution)/shard_map/pallas_call | solution.py:337
  51.8 1.7 %copy.7 = bf16[24,5120]{1,0:T(8,128)(2,1)} copy(bf16[24,5120]{1,0:T(8,128)(2,1)} %shard_map.55) | data formatting | bytes 491520

commit v4 on v3

--- a/solution.py
+++ b/solution.py
@@ -65,14 +65,13 @@
     ("attend", 0, 0, 3),
     ("take", 1, (0, -2), (1, -3)),
     ("project", 0),
+    ("attend", 1, 0, 2),
+    ("attend", 1, 0, 3),
     ("take", 1, (0, -3), (1, 4), (1, 1), (1, 2)),
     ("attend", 1, 1, 1),
+    ("through", 0, 0, 1, 2, 3),
     ("attend", 1, 1, 2),
     ("attend", 1, 1, 3),
-    ("attend", 1, 0, 2),
-    ("through", 0, 0, 1),
-    ("attend", 1, 0, 3),
-    ("through", 0, 2, 3),
     ("cross", 0, 0, 1, 2, 3),
     ("project", 1),
 ]

time: 53.6 us -> 54.3 us (1.013)
  Pallas kernels: 51.8 us -> 52.5 us
    pallas_call x1, Pallas kernels: 51.8 us -> 52.5 us  [shards(): pl.pallas_call(kernel, out_shape=jax.ShapeDtypeStruct((OWN, 2 * HALF), jn...]
where the time goes in v4:
time: 54.3 us; the launch traced here: 54.2 us
  Pallas kernels  52.5 us (97%)
  local copies, waits for them, and re-layouts  1.65 us (3%)
    pallas_call x1, Pallas kernels, shards(): pl.pallas_call(kernel, out_shape=jax.ShapeDtypeStruct((OWN, 2 * HALF), jn...  52.5 us
    unnamed x1, local copies, waits for them, and re-layouts  1.65 us

profile of v4, /device:TPU:24, one launch (start us, length us, event | category | flops | bytes accessed | tf_op | source)
XLA Modules:
  0.0 54.2 jit_solution(5992168507666232672)
XLA Ops:
  0.0 52.5 %shard_map.55 = bf16[24,5120]{1,0:T(8,128)(2,1)} custom-call(bf16[192,640]{1,0:T(8,128)(2,1)} %q_hbm.1, bf16[192,128]{1,0:T(8,128)(2,1)} %k_hbm.1, bf16[192,128]{1,0:T(8,128)(2,1)} %v_hbm.1, s32[192]{0:T(256)} %pos_hbm.1, bf16[640,5120]{1,0:T(8,128)(2,1)} %w_hbm.1), custom_call_target="tpu_custom_call" | custom-call | flops 4000000000 | bytes 10000000 | tf_op jit(solution)/shard_map/pallas_call | solution.py:336
  52.6 1.7 %copy.7 = bf16[24,5120]{1,0:T(8,128)(2,1)} copy(bf16[24,5120]{1,0:T(8,128)(2,1)} %shard_map.55) | data formatting | bytes 491520

commit v5 on v3

--- a/solution.py
+++ b/solution.py
@@ -62,11 +62,11 @@
     ("take", 1, (0, 4)),
     ("attend", 1, 0, 1),
     ("take", 1, (1, 3), (0, 1)),
+    ("attend", 1, 1, 1),
     ("attend", 0, 0, 3),
     ("take", 1, (0, -2), (1, -3)),
     ("project", 0),
     ("take", 1, (0, -3), (1, 4), (1, 1), (1, 2)),
-    ("attend", 1, 1, 1),
     ("attend", 1, 1, 2),
     ("attend", 1, 1, 3),
     ("attend", 1, 0, 2),

time: 53.6 us -> 55 us (1.026)
  Pallas kernels: 51.8 us -> 52.9 us
    pallas_call x1, Pallas kernels: 51.8 us -> 52.9 us  [shards(): pl.pallas_call(kernel, out_shape=jax.ShapeDtypeStruct((OWN, 2 * HALF), jn...]
where the time goes in v5:
time: 55 us; the launch traced here: 54.6 us
  Pallas kernels  52.9 us (96%)
  local copies, waits for them, and re-layouts  1.65 us (3%)
    pallas_call x1, Pallas kernels, shards(): pl.pallas_call(kernel, out_shape=jax.ShapeDtypeStruct((OWN, 2 * HALF), jn...  52.9 us
    unnamed x1, local copies, waits for them, and re-layouts  1.65 us

profile of v5, /device:TPU:24, one launch (start us, length us, event | category | flops | bytes accessed | tf_op | source)
XLA Modules:
  0.0 54.6 jit_solution(1357513858613558213)
XLA Ops:
  0.0 52.9 %shard_map.55 = bf16[24,5120]{1,0:T(8,128)(2,1)} custom-call(bf16[192,640]{1,0:T(8,128)(2,1)} %q_hbm.1, bf16[192,128]{1,0:T(8,128)(2,1)} %k_hbm.1, bf16[192,128]{1,0:T(8,128)(2,1)} %v_hbm.1, s32[192]{0:T(256)} %pos_hbm.1, bf16[640,5120]{1,0:T(8,128)(2,1)} %w_hbm.1), custom_call_target="tpu_custom_call" | custom-call | flops 4000000000 | bytes 10000000 | tf_op jit(solution)/shard_map/pallas_call | solution.py:337
  52.9 1.7 %copy.7 = bf16[24,5120]{1,0:T(8,128)(2,1)} copy(bf16[24,5120]{1,0:T(8,128)(2,1)} %shard_map.55) | data formatting | bytes 491520

commit v6 on v3

--- a/solution.py
+++ b/solution.py
@@ -68,11 +68,10 @@
     ("take", 1, (0, -3), (1, 4), (1, 1), (1, 2)),
     ("attend", 1, 1, 1),
     ("attend", 1, 1, 2),
+    ("through", 0, 0, 1, 2, 3),
     ("attend", 1, 1, 3),
     ("attend", 1, 0, 2),
-    ("through", 0, 0, 1),
     ("attend", 1, 0, 3),
-    ("through", 0, 2, 3),
     ("cross", 0, 0, 1, 2, 3),
     ("project", 1),
 ]

time: 53.6 us -> 54.8 us (1.022)
  Pallas kernels: 51.8 us -> 53.1 us
    pallas_call x1, Pallas kernels: 51.8 us -> 53.1 us  [shards(): pl.pallas_call(kernel, out_shape=jax.ShapeDtypeStruct((OWN, 2 * HALF), jn...]
where the time goes in v6:
time: 54.8 us; the launch traced here: 54.7 us
  Pallas kernels  53.1 us (97%)
  local copies, waits for them, and re-layouts  1.65 us (3%)
    pallas_call x1, Pallas kernels, shards(): pl.pallas_call(kernel, out_shape=jax.ShapeDtypeStruct((OWN, 2 * HALF), jn...  53.1 us
    unnamed x1, local copies, waits for them, and re-layouts  1.65 us

profile of v6, /device:TPU:24, one launch (start us, length us, event | category | flops | bytes accessed | tf_op | source)
XLA Modules:
  0.0 54.7 jit_solution(11664278127836086958)
XLA Ops:
  0.0 53.1 %shard_map.55 = bf16[24,5120]{1,0:T(8,128)(2,1)} custom-call(bf16[192,640]{1,0:T(8,128)(2,1)} %q_hbm.1, bf16[192,128]{1,0:T(8,128)(2,1)} %k_hbm.1, bf16[192,128]{1,0:T(8,128)(2,1)} %v_hbm.1, s32[192]{0:T(256)} %pos_hbm.1, bf16[640,5120]{1,0:T(8,128)(2,1)} %w_hbm.1), custom_call_target="tpu_custom_call" | custom-call | flops 4000000000 | bytes 10000000 | tf_op jit(solution)/shard_map/pallas_call | solution.py:336
  53.1 1.7 %copy.7 = bf16[24,5120]{1,0:T(8,128)(2,1)} copy(bf16[24,5120]{1,0:T(8,128)(2,1)} %shard_map.55) | data formatting | bytes 491520
